TPU v7x, 32 devices: a whole 2x2x4 slice. The times are simulated.
32 devices in a mesh: site: 8 (over z, y), branch: 4 (over x, core).
Axes of the slice: x: 2, y: 2, z: 4, core: 2. Of those that a mesh axis runs over, the one named last changes fastest.
Arguments:
- states: int32 [256, 2048], P(None, 'site'), may hold values from 0 to 63, as said below
- gap_mask: int32 [256, 2048], P(None, 'site'), may hold values 0 or 1
- weights: int32 [2048], P('site'), may hold values from 1 to 9
- leaf_order: int32 [256], replicated, may hold values from 0 to 255, each once
- exchanges: float32 [64, 64], replicated, may hold values from 0.3 to 3
- codon_freq: float32 [64], replicated, may hold values from 0.3 to 3
- omega_ratio: float32 [8], replicated, may hold values from 0.1 to 2
- lengths: float32 [508], P('branch'), may hold values from 0.05 to 1.5
- classes: int32 [508], P('branch'), may hold values from 0 to 7
Outputs:
- grad_exch: float32 [64, 64], replicated
- grad_omega: float32 [8], replicated
- grad_length: float32 [508], P('branch')
- loglik: float32 [], replicated
Inputs may be any that keep to these rules, and one draw needn't show every extreme that they name: `states`: every state is a sense codon: never 10, 11 or 14.
All inputs are finite; a program needn't handle non-finite values. No bound on the sum of `gap_mask` on one device may be relied on, other than what follows from the above.
Results may differ from a plain program's by a relative error of at most 0.0003.
Values sent between devices are 32-bit elements; how exact they have to be, the bound alone decides.
No kernel may reach another device: no remote copies, remote signals or barrier semaphores. Data moves between devices by JAX's collectives and lax.ppermute only.
A program may use at most 192 MiB of HBM per device.

v0:
```python
import functools
import jax
import jax.numpy as jnp
import numpy as np
from jax import lax
from jax.experimental import pallas as pl
from jax.experimental.pallas import tpu as pltpu
from jax.sharding import PartitionSpec as P

LEAF_DEV = 64
EDGES = 127
PAIRS = 64
CLASSES = 8
ORDER = 8
BF = jnp.bfloat16
F32 = jnp.float32

CODE_TABLE = "FFLLSSSSYYXXCCXWLLLLPPPPHHQQRRRRIIIMTTTTNNKKSSRRVVVVAAAADDEEGGGG"


def codon_tables():
    amino_acid = np.array(list(CODE_TABLE))
    codon_index = np.arange(64)
    digits = np.stack([codon_index // 16, codon_index // 4 % 4, codon_index % 4], 1)
    differ = (digits[:, None, :] != digits[None, :, :]).sum(-1)
    is_sense = amino_acid != "X"
    single = (differ == 1) & is_sense[:, None] & is_sense[None, :]
    nonsyn = single & (amino_acid[:, None] != amino_acid[None, :])
    return (is_sense.astype(np.float32), single.astype(np.float32), nonsyn.astype(np.float32))


def low_half():
    return lax.broadcasted_iota(jnp.int32, (64, 128), 1) < 64


def split(x):
    high = x.astype(BF)
    low = (x - high.astype(F32)).astype(BF)
    return high, low


def spread(x):
    mask = low_half()
    zero = jnp.zeros_like(x)
    return jnp.concatenate([jnp.where(mask, x, zero), jnp.where(mask, zero, x)], axis=0)


def mxu(left, right):
    return jnp.dot(left, right, preferred_element_type=F32)


def mxu_nt(left, right):
    return lax.dot_general(left, right, (((1,), (1,)), ((), ())), preferred_element_type=F32)


def exact(left, right):
    return jnp.dot(left, right, preferred_element_type=F32, precision=lax.Precision.HIGHEST)


def exact_tn(left, right):
    return lax.dot_general(
        left, right, (((0,), (0,)), ((), ())), preferred_element_type=F32,
        precision=lax.Precision.HIGHEST,
    )


def pair_products(*terms):
    lefts, rights = [], []
    for left, right in terms:
        left_high, left_low = split(left)
        right_high, right_low = split(right)
        wide_high, wide_low = spread(right_high), spread(right_low)
        lefts += [left_high, left_high, left_low]
        rights += [wide_high, wide_low, wide_high]
    return mxu(jnp.concatenate(lefts, axis=1), jnp.concatenate(rights, axis=0))


def per_pair_messages(matrix, high, low):
    matrix_high, matrix_low = split(matrix)
    wide_high, wide_low = spread(matrix_high), spread(matrix_low)
    if low is None:
        return mxu(
            jnp.concatenate([wide_high, wide_low], axis=1), jnp.concatenate([high, high], axis=0)
        )
    return mxu(
        jnp.concatenate([wide_high, wide_high, wide_low], axis=1),
        jnp.concatenate([high, low, high], axis=0),
    )


def frequencies(freq_ref, sense_ref):
    row = lax.broadcasted_iota(jnp.int32, (64, 128), 0)
    lane = lax.broadcasted_iota(jnp.int32, (64, 128), 1)
    twice = (row == lane % 64).astype(F32)
    sense2 = sense_ref[...]
    freq2 = exact(jnp.broadcast_to(freq_ref[...], (8, 64)), twice)[0:1] * sense2
    total = 0.5 * jnp.sum(freq2, axis=1, keepdims=True)
    pi_row = freq2 / total
    pi_col = 0.5 * jnp.sum(twice * pi_row, axis=1, keepdims=True)
    sense_col = 0.5 * jnp.sum(twice * sense2, axis=1, keepdims=True)
    root_row = jnp.sqrt(jnp.where(sense2 > 0, pi_row, 1.0))
    root_col = jnp.sqrt(jnp.where(sense_col > 0, pi_col, 1.0))
    return twice, pi_row, pi_col, root_row, root_col


def symmetric_table(ex_ref, single_ref, twice):
    ex = ex_ref[...]
    return 0.5 * (exact(ex, twice) + exact_tn(ex, twice)) * single_ref[...]


def class_pair(table, nonsyn, omega_ref, pair, twice, pi_row, pi_col):
    mask = low_half()
    omega = jnp.where(mask, omega_ref[2 * pair], omega_ref[2 * pair + 1])
    factor = 1.0 + nonsyn * (omega - 1.0)
    flux = table * factor
    off = flux * pi_row
    row0 = jnp.sum(jnp.where(mask, off, 0.0), axis=1, keepdims=True)
    row1 = jnp.sum(jnp.where(mask, 0.0, off), axis=1, keepdims=True)
    mean0 = jnp.sum(pi_col * row0, axis=0, keepdims=True)
    mean1 = jnp.sum(pi_col * row1, axis=0, keepdims=True)
    rows = jnp.where(mask, row0, row1)
    mean = jnp.where(mask, mean0, mean1)
    return factor, off, rows, mean


def neighbours():
    row = lax.broadcasted_iota(jnp.int32, (64, 128), 0)
    lane = lax.broadcasted_iota(jnp.int32, (64, 128), 1) % 64
    masks = [
        row % 16 == lane % 16,
        (row // 16 == lane // 16) & (row % 4 == lane % 4),
        row // 4 == lane // 4,
    ]
    codon = lax.broadcasted_iota(jnp.int32, (64, 16), 0)
    column = lax.broadcasted_iota(jnp.int32, (64, 16), 1)
    digits = [codon // 16, codon // 4 % 4, codon % 4]
    picks = [(column == 4 * p + digits[p]).astype(F32) for p in range(3)]
    return masks, picks


def up_kernel(
    states_ref, gap_ref, order_ref, ex_ref, freq_ref, omega_ref, len_ref, cls_ref,
    sense_ref, single_ref, nonsyn_ref,
    top_ref, chain_ref, slope_ref, power_ref, message_ref, high_ref, low_ref, leaf_ref,
    scale_ref, inverse_ref, dup_ref,
):
    subtree = lax.axis_index("branch")
    mask = low_half()
    twice, pi_row, pi_col, root_row, root_col = frequencies(freq_ref, sense_ref)
    table = symmetric_table(ex_ref, single_ref, twice)
    nonsyn = nonsyn_ref[...]

    powers = []
    for pair in range(CLASSES // 2):
        factor, off, rows, mean = class_pair(
            table, nonsyn, omega_ref, pair, twice, pi_row, pi_col
        )
        powers.append([(table * factor * root_col * root_row - twice * rows) / mean])
    for left, right in ((0, 0), (1, 0), (1, 1), (3, 0), (3, 1), (3, 2), (3, 3)):
        for pair in range(CLASSES // 2):
            powers[pair].append(pair_products((powers[pair][left], powers[pair][right])))
    for pair in range(CLASSES // 2):
        for k in range(ORDER):
            value = powers[pair][k]
            swapped = pltpu.roll(value, 64, 1)
            dup_ref[2 * pair, k] = jnp.where(mask, value, swapped)
            dup_ref[2 * pair + 1, k] = jnp.where(mask, swapped, value)
            if k < 4:
                power_ref[pair, k] = value

    def exponentials(step, carry):
        held = []
        for j in range(8):
            p = step * 8 + j
            odd = jnp.minimum(2 * p + 1, EDGES - 1)
            y0 = len_ref[2 * p] * 0.0625
            y1 = jnp.where(2 * p + 1 < EDGES, len_ref[odd] * 0.0625, 0.0)
            c0, c1 = cls_ref[2 * p], cls_ref[odd]
            y = jnp.where(lax.broadcasted_iota(jnp.int32, (8, 128), 1) < 64, y0, y1)
            slope_coef = jnp.ones_like(y)
            value = slope = None
            for k in range(ORDER):
                coef = slope_coef * y * (1.0 / (k + 1))
                matrix = jnp.where(mask, dup_ref[c0, k], dup_ref[c1, k])
                first, second = matrix * coef[0:1], matrix * slope_coef[0:1]
                value = first if k == 0 else value + first
                slope = second if k == 0 else slope + second
                slope_coef = coef
            chain_ref[0, p] = value
            slope_ref[p] = slope
            held.append(value)
        for level in range(4):
            for j in range(8):
                held[j] = 2.0 * held[j] + pair_products((held[j], held[j]))
                chain_ref[level + 1, step * 8 + j] = held[j]
        return carry

    lax.fori_loop(0, PAIRS // 8, exponentials, 0)

    eye2 = twice
    inverse_root_col = 1.0 / root_col

    def transition(p):
        return inverse_root_col * (chain_ref[4, p] + eye2) * root_row

    def finish(p, message):
        message_ref[p] = message
        raw = message[0:64] * message[64:128]
        scaling = jnp.sum(raw, axis=0, keepdims=True)
        inverse = 1.0 / scaling
        scale_ref[pl.ds(p, 1), :] = scaling
        inverse_ref[pl.ds(p, 1), :] = inverse
        high, low = split(raw * inverse)
        high_ref[p] = high
        low_ref[p] = low

    sites = states_ref.shape[1]
    codon = lax.broadcasted_iota(jnp.int32, (64, sites), 0)

    def leaf_level(step, carry):
        for j in range(4):
            p = step * 4 + j
            both = []
            for e in range(2):
                taxon = order_ref[subtree * LEAF_DEV + 2 * p + e]
                state = jnp.where(
                    gap_ref[pl.ds(taxon, 1), :] > 0, -1, states_ref[pl.ds(taxon, 1), :]
                )
                hit = (codon == state) | (state < 0)
                both.append(jnp.where(hit, 1.0, 0.0).astype(BF))
            leaves = jnp.concatenate(both, axis=0)
            leaf_ref[p] = leaves
            finish(p, per_pair_messages(transition(p), leaves, None))
        return carry

    lax.fori_loop(0, LEAF_DEV // 8, leaf_level, 0)

    def inner(p):
        child = 2 * p - 64
        high = jnp.concatenate([high_ref[child], high_ref[child + 1]], axis=0)
        low = jnp.concatenate([low_ref[child], low_ref[child + 1]], axis=0)
        return per_pair_messages(transition(p), high, low)

    def second_level(step, carry):
        for j in range(4):
            finish(32 + step * 4 + j, inner(32 + step * 4 + j))
        return carry

    lax.fori_loop(0, 4, second_level, 0)
    for p in range(48, 63):
        finish(p, inner(p))
    high_ref[63] = jnp.zeros((64, sites), BF)
    low_ref[63] = jnp.zeros((64, sites), BF)
    scale_ref[63:64, :] = jnp.ones((1, sites), F32)
    inverse_ref[63:64, :] = jnp.ones((1, sites), F32)
    top = inner(63)
    message_ref[63] = top
    top_ref[...] = top[0:64]


def down_kernel(
    total_sites,
    tops_ref, chain_ref, slope_ref, power_ref, message_ref, high_ref, low_ref, leaf_ref,
    scale_ref, inverse_ref, weights_ref, ex_ref, freq_ref, omega_ref, len_ref, cls_ref,
    sense_ref, single_ref, nonsyn_ref,
    out_ref,
    a_high_ref, a_low_ref, count_ref, bins_ref, dot_ref,
):
    subtree = lax.axis_index("branch")
    members = lax.axis_size("branch")
    mask = low_half()
    twice, pi_row, pi_col, root_row, root_col = frequencies(freq_ref, sense_ref)
    inverse_root_row, inverse_root_col = 1.0 / root_row, 1.0 / root_col
    sites = weights_ref.shape[1]
    weight = weights_ref[...].astype(F32)

    above = jnp.broadcast_to(pi_col, (64, sites))
    own = jnp.zeros((64, sites), F32)
    for member in range(members):
        message = tops_ref[member * 64 : member * 64 + 64, :]
        above = jnp.where(subtree == member, above, above * message)
        own = jnp.where(subtree == member, message, own)
    likelihood = jnp.sum(above * own, axis=0, keepdims=True)
    logs = jnp.sum(jnp.log(scale_ref[...]), axis=0, keepdims=True)
    logs = logs + jnp.where(subtree == 0, jnp.log(likelihood), 0.0)
    log_part = jnp.sum(weight * logs, axis=1, keepdims=True)
    high, low = split(above * (weight / (likelihood * total_sites)))
    a_high_ref[31, 0:64, :] = high
    a_low_ref[31, 0:64, :] = low
    a_high_ref[31, 64:128, :] = jnp.zeros((64, sites), BF)
    a_low_ref[31, 64:128, :] = jnp.zeros((64, sites), BF)

    eye2 = twice

    def store_counts(p, square):
        counts = jnp.where(mask, square[0:64], square[64:128])
        count_ref[p] = inverse_root_col * counts * root_row

    def descend(r):
        a_high, a_low = a_high_ref[r - 32], a_low_ref[r - 32]
        child = 2 * r - 64
        u_high = jnp.concatenate([high_ref[child], high_ref[child + 1]], axis=0)
        u_low = jnp.concatenate([low_ref[child], low_ref[child + 1]], axis=0)
        first = mxu_nt(a_high, jnp.concatenate([u_high, u_low], axis=0))
        second = mxu_nt(a_low, u_high)
        store_counts(r, first[:, 0:128] + first[:, 128:256] + second)
        matrix = root_col * (chain_ref[4, r] + eye2) * inverse_root_row
        return per_pair_messages(matrix, a_high, a_low)

    def children(down, e, p):
        vector = down[64 * e : 64 * e + 64]
        inverse = inverse_ref[pl.ds(p, 1), :]
        message = message_ref[p]
        pair = jnp.concatenate(
            [vector * message[64:128] * inverse, vector * message[0:64] * inverse], axis=0
        )
        return split(pair)

    def inner(r):
        down = descend(r)
        for e in range(2):
            p = 2 * r + e - 64
            if isinstance(p, int) and p == 63:
                continue
            high, low = children(down, e, p)
            a_high_ref[p - 32] = high
            a_low_ref[p - 32] = low

    for r in range(63, 47, -1):
        inner(r)

    def leaf_level(step, carry):
        for j in range(2):
            r = 32 + step * 2 + j
            down = descend(r)
            for e in range(2):
                p = 2 * r + e - 64
                high, low = children(down, e, p)
                square = mxu_nt(jnp.concatenate([high, low], axis=0), leaf_ref[p])
                store_counts(p, square[0:128] + square[128:256])
        return carry

    lax.fori_loop(0, 8, leaf_level, 0)

    bins_ref[...] = jnp.zeros_like(bins_ref)

    def adjoint(step, carry):
        held = [count_ref[step * 8 + j] for j in range(8)]
        for level in range(3, -1, -1):
            for j in range(8):
                matrix = chain_ref[level, step * 8 + j]
                held[j] = 2.0 * held[j] + pair_products((held[j], matrix), (matrix, held[j]))
        for j in range(8):
            p = step * 8 + j
            odd = jnp.minimum(2 * p + 1, EDGES - 1)
            y0 = len_ref[2 * p] * 0.0625
            y1 = jnp.where(2 * p + 1 < EDGES, len_ref[odd] * 0.0625, 0.0)
            c0, c1 = cls_ref[2 * p], cls_ref[odd]
            y = jnp.where(lax.broadcasted_iota(jnp.int32, (8, 128), 1) < 64, y0, y1)
            dot_ref[p] = jnp.sum((held[j] * slope_ref[p]).reshape(8, 8, 128), axis=0)
            even = jnp.where(mask, held[j], 0.0)
            other = jnp.where(mask, 0.0, held[j])
            coef = jnp.ones_like(y)
            for k in range(ORDER):
                coef = coef * y * (1.0 / (k + 1))
                bins_ref[c0, k] += even * coef[0:1]
                bins_ref[c1, k] += other * coef[0:1]
        return carry

    lax.fori_loop(0, PAIRS // 8, adjoint, 0)

    table = symmetric_table(ex_ref, single_ref, twice)
    nonsyn = nonsyn_ref[...]
    row = lax.broadcasted_iota(jnp.int32, (64, 128), 0)
    lane = lax.broadcasted_iota(jnp.int32, (64, 128), 1)
    table_grad = jnp.zeros((64, 128), F32)
    omega_row = jnp.zeros((1, 128), F32)
    lane_row = lax.broadcasted_iota(jnp.int32, (1, 128), 1)
    for pair in range(CLASSES // 2):
        grads = []
        for k in range(ORDER):
            first, second = bins_ref[2 * pair, k], bins_ref[2 * pair + 1, k]
            first = first + pltpu.roll(first, 64, 1)
            second = second + pltpu.roll(second, 64, 1)
            grads.append(jnp.where(mask, first, second))
        g1, g2, g3, g4, g5, g6, g7, g8 = grads
        a1, a2, a3, a4 = [power_ref[pair, k] for k in range(4)]
        g4 = g4 + pair_products((g8, a4), (a4, g8), (g7, a3), (g6, a2), (g5, a1))
        g3 = g3 + pair_products((a4, g7))
        g2 = g2 + pair_products((a4, g6))
        g1 = g1 + pair_products((a4, g5))
        g2 = g2 + pair_products((g4, a2), (a2, g4), (g3, a1))
        g1 = g1 + pair_products((a2, g3))
        g1 = g1 + pair_products((g2, a1), (a1, g2))
        factor, off, rows, mean = class_pair(
            table, nonsyn, omega_ref, pair, twice, pi_row, pi_col
        )
        d_rate = root_col * g1 * inverse_root_row
        rate = (off - twice * rows) / mean
        weighted = d_rate * rate
        diagonal = d_rate * twice
        total0 = jnp.sum(jnp.where(mask, weighted, 0.0), axis=1, keepdims=True)
        total1 = jnp.sum(jnp.where(mask, 0.0, weighted), axis=1, keepdims=True)
        total0 = jnp.sum(total0, axis=0, keepdims=True)
        total1 = jnp.sum(total1, axis=0, keepdims=True)
        diag0 = jnp.sum(jnp.where(mask, diagonal, 0.0), axis=1, keepdims=True)
        diag1 = jnp.sum(jnp.where(mask, 0.0, diagonal), axis=1, keepdims=True)
        row_grad = jnp.where(mask, diag0 + pi_col * total0, diag1 + pi_col * total1)
        flux_grad = (d_rate - row_grad) * pi_row / mean
        table_grad = table_grad + flux_grad * factor * single_ref[...]
        ratio = flux_grad * table * nonsyn
        ratio0 = jnp.sum(jnp.where(mask, ratio, 0.0), axis=1, keepdims=True)
        ratio1 = jnp.sum(jnp.where(mask, 0.0, ratio), axis=1, keepdims=True)
        ratio0 = jnp.sum(ratio0, axis=0, keepdims=True)
        ratio1 = jnp.sum(ratio1, axis=0, keepdims=True)
        omega_row = jnp.where(lane_row == 2 * pair, ratio0, omega_row)
        omega_row = jnp.where(lane_row == 2 * pair + 1, ratio1, omega_row)
    table_grad = table_grad + pltpu.roll(table_grad, 64, 1)
    one = table_grad[:, 0:64]
    both = 0.5 * (exact(one, twice) + exact_tn(one, twice))
    masks, picks = neighbours()
    packed = jnp.zeros((16, 128), F32)
    for at_position, pick in zip(masks, picks):
        packed = packed + exact_tn(pick, jnp.where(at_position, both, 0.0))
    packed = jnp.where(lax.broadcasted_iota(jnp.int32, (16, 128), 1) < 64, packed, 0.0)

    slopes = jnp.sum(dot_ref[...], axis=1) * 0.0625
    even = jnp.sum(jnp.where(mask, slopes, 0.0), axis=1, keepdims=True)
    other = jnp.sum(jnp.where(mask, 0.0, slopes), axis=1, keepdims=True)
    placed = jnp.where(lane == 2 * row, even, 0.0) + jnp.where(lane == 2 * row + 1, other, 0.0)
    length_row = jnp.sum(placed, axis=0, keepdims=True)
    line = lax.broadcasted_iota(jnp.int32, out_ref.shape, 0)
    omega_row = jnp.where(lane_row == CLASSES, log_part, omega_row)
    omega_row = pltpu.roll(jnp.broadcast_to(omega_row, (8, 128)), 64, 1)[0:1]
    packed = packed + jnp.where(line == 0, omega_row, 0.0)
    out_ref[...] = packed + jnp.where(line == 12 + subtree, length_row, 0.0)


def last_kernel(total_sites, parts_ref, exch_ref, omega_ref, length_ref, log_ref):
    members = lax.axis_size("branch")
    subtree = lax.axis_index("branch")
    devices = parts_ref.shape[0]
    total = parts_ref[0]
    for device in range(1, devices):
        total = total + parts_ref[device]
    masks, picks = neighbours()
    table = jnp.zeros((64, 128), F32)
    for at_position, pick in zip(masks, picks):
        table = table + jnp.where(at_position, exact(pick, total), 0.0)
    exch_ref[...] = table[:, 0:64]
    moved = pltpu.roll(total[0:8], 64, 1)
    omega_ref[...] = moved[0:1, 0:CLASSES]
    line = lax.broadcasted_iota(jnp.int32, total.shape, 0)
    lengths = jnp.sum(jnp.where(line == 12 + subtree, total, 0.0), axis=0, keepdims=True)
    length_ref[...] = lengths[:, 0:EDGES]
    log_ref[...] = moved[0:1, CLASSES : CLASSES + 1] / total_sites / (LEAF_DEV * members)


def body(
    total_sites, states, gap_mask, weights, leaf_order, exchanges, codon_freq, omega_ratio,
    lengths, classes,
):
    sites = states.shape[1]
    members = lax.axis_size("branch")
    sense, single, nonsyn = codon_tables()
    sense2 = jnp.asarray(np.tile(sense[None, :], (1, 2)))
    single2 = jnp.asarray(np.tile(single, (1, 2)))
    nonsyn2 = jnp.asarray(np.tile(nonsyn, (1, 2)))
    freq = codon_freq.reshape(1, 64)
    vmem = pl.BlockSpec(memory_space=pltpu.VMEM)
    smem = pl.BlockSpec(memory_space=pltpu.SMEM)
    shape = jax.ShapeDtypeStruct
    held = pltpu.VMEM
    top, *kept = pl.pallas_call(
        up_kernel,
        out_shape=[
            shape((64, sites), F32),
            held((5, PAIRS, 64, 128), F32),
            held((PAIRS, 64, 128), F32),
            held((CLASSES // 2, 4, 64, 128), F32),
            held((PAIRS, 128, sites), F32),
            held((64, 64, sites), BF),
            held((64, 64, sites), BF),
            held((32, 128, sites), BF),
            held((64, sites), F32),
            held((64, sites), F32),
        ],
        in_specs=[vmem, vmem, smem, vmem, vmem, smem, smem, smem, vmem, vmem, vmem],
        out_specs=[vmem] * 10,
        scratch_shapes=[pltpu.VMEM((CLASSES, ORDER, 64, 128), F32)],
        compiler_params=pltpu.CompilerParams(vmem_limit_bytes=28 * 2**20),
        name="up",
    )(
        states, gap_mask, leaf_order, exchanges, freq, omega_ratio, lengths, classes,
        sense2, single2, nonsyn2,
    )
    kept = [pltpu.with_memory_space_constraint(x, pltpu.VMEM) for x in kept]
    tops = lax.all_gather(top, "branch", axis=0, tiled=True)
    part = pl.pallas_call(
        functools.partial(down_kernel, total_sites),
        out_shape=shape((16, 128), F32),
        in_specs=[vmem] * 13 + [smem] * 3 + [vmem] * 3,
        out_specs=vmem,
        scratch_shapes=[
            pltpu.VMEM((32, 128, sites), BF),
            pltpu.VMEM((32, 128, sites), BF),
            pltpu.VMEM((PAIRS, 64, 128), F32),
            pltpu.VMEM((CLASSES, ORDER, 64, 128), F32),
            pltpu.VMEM((PAIRS, 8, 128), F32),
        ],
        compiler_params=pltpu.CompilerParams(vmem_limit_bytes=28 * 2**20),
        name="down",
    )(
        tops, *kept, weights.reshape(1, sites), exchanges, freq, omega_ratio, lengths, classes,
        sense2, single2, nonsyn2,
    )
    parts = lax.all_gather(part, ("site", "branch"), axis=0)
    exch, omega, length, loglik = pl.pallas_call(
        functools.partial(last_kernel, total_sites),
        out_shape=[shape((64, 64), F32), shape((1, CLASSES), F32), shape((1, EDGES), F32), shape((1, 1), F32)],
        in_specs=[vmem],
        out_specs=[vmem] * 4,
        compiler_params=pltpu.CompilerParams(vmem_limit_bytes=24 * 2**20),
        name="last",
    )(parts)
    return (exch, omega.reshape(CLASSES), length.reshape(EDGES), loglik.reshape(()))


def solution(mesh):
    def whole(states, *rest):
        total_sites = states.shape[1]
        return jax.shard_map(
            functools.partial(body, total_sites),
            mesh=mesh,
            in_specs=(
                P(None, "site"),
                P(None, "site"),
                P("site"),
                P(),
                P(),
                P(),
                P(),
                P("branch"),
                P("branch"),
            ),
            out_specs=(P(), P(), P("branch"), P()),
            check_vma=False,
        )(states, *rest)

    return whole
```

profile of v0, /device:TPU:0, one launch (start us, length us, event | category | flops | bytes accessed | tf_op | source)
XLA Modules:
  0.0 96.3 jit_solution(4772474698781890172)
XLA Ops:
  0.6 19.5 %up.1 = (f32[64,256]{1,0:T(8,128)}, f32[5,64,64,128]{3,2,1,0:T(8,128)S(1)}, f32[64,64,128]{2,1,0:T(8,128)S(1)}, f32[4,4,64,128]{3,2,1,0:T(8,128)S(1)}, f32[64,12...) custom-call(s32[256,256]{1,0:T(8,128)} %states_ref.1, ...), custom_call_target="tpu_custom_call" | custom-call | tf_op jit(solution)/shard_map/up/pallas_call | solution.py:474
  20.1 8.8 %all_gather.9.tops_ref = f32[256,256]{1,0:T(8,128)} all-gather(f32[64,256]{1,0:T(8,128)} %get-tuple-element.18), channel_id=1, replica_groups=mesh['site'=8,'branch'=4] {'branch'}, dimensions={0}, use_global_device_ids=true | all-gather | bytes 327680 | tf_op jit(solution)/shard_map/all_gather | solution.py:498
  28.9 24.8 %down.1 = f32[16,128]{1,0:T(8,128)} custom-call(f32[256,256]{1,0:T(8,128)} %all_gather.9.tops_ref, f32[5,64,64,128]{3,2,1,0:T(8,128)S(1)} %get-tuple-element.19.chain_ref, f32[64,64,128]{2,1,0:T(8,128)S(1)} %get-tuple-element.20.slope_ref, f32[4,4,64,128]{3,2,1,0:T(8,128)S(1)} %get-tuple-element.21.power_ref, ...), custom_call_target="tpu_custom_call" | custom-call | tf_op jit(solution)/shard_map/down/pallas_call | solution.py:499
  53.7 41.8 %all-gather = f32[512,128]{1,0:T(8,128)S(1)} all-gather(f32[16,128]{1,0:T(8,128)} %down.1), channel_id=2, replica_groups=mesh['site'=8,'branch'=4] {'site','branch'}, dimensions={0}, use_global_device_ids=true | all-gather | bytes 270336 | tf_op jit(solution)/shard_map/all_gather | solution.py:517
  95.5 0.9 last.1
where the time goes:
time: 96.6 us; the launch traced here: 96.3 us
  blocking collectives  50.6 us (52%)
  Pallas kernels  45.1 us (47%)
    all_gather x1, blocking collectives, body(): parts = lax.all_gather(part, ('site', 'branch'), axis=0)  41.8 us
    pallas_call x1, Pallas kernels, body(): pl.pallas_call(functools.partial(down_kernel, total_sites), out_shape=sha...  24.8 us
    pallas_call x1, Pallas kernels, body(): pl.pallas_call(up_kernel, out_shape=[shape((64, sites), F32), held((5, PA...  19.5 us
    all_gather x1, blocking collectives, body(): tops = lax.all_gather(top, 'branch', axis=0, tiled=True)  8.79 us

commit v1 on v0

--- a/solution.py
+++ b/solution.py
@@ -258,16 +258,16 @@
     top_ref[...] = top[0:64]
 
 
-def down_kernel(
-    total_sites,
-    tops_ref, chain_ref, slope_ref, power_ref, message_ref, high_ref, low_ref, leaf_ref,
+def down_kernel(total_sites, members, *refs):
+    tops, refs = refs[:members], refs[members:]
+    (
+        chain_ref, slope_ref, power_ref, message_ref, high_ref, low_ref, leaf_ref,
     scale_ref, inverse_ref, weights_ref, ex_ref, freq_ref, omega_ref, len_ref, cls_ref,
     sense_ref, single_ref, nonsyn_ref,
     out_ref,
     a_high_ref, a_low_ref, count_ref, bins_ref, dot_ref,
-):
+    ) = refs
     subtree = lax.axis_index("branch")
-    members = lax.axis_size("branch")
     mask = low_half()
     twice, pi_row, pi_col, root_row, root_col = frequencies(freq_ref, sense_ref)
     inverse_root_row, inverse_root_col = 1.0 / root_row, 1.0 / root_col
@@ -275,11 +275,9 @@
     weight = weights_ref[...].astype(F32)
 
     above = jnp.broadcast_to(pi_col, (64, sites))
-    own = jnp.zeros((64, sites), F32)
-    for member in range(members):
-        message = tops_ref[member * 64 : member * 64 + 64, :]
-        above = jnp.where(subtree == member, above, above * message)
-        own = jnp.where(subtree == member, message, own)
+    for other in tops[1:]:
+        above = above * other[...]
+    own = tops[0][...]
     likelihood = jnp.sum(above * own, axis=0, keepdims=True)
     logs = jnp.sum(jnp.log(scale_ref[...]), axis=0, keepdims=True)
     logs = logs + jnp.where(subtree == 0, jnp.log(likelihood), 0.0)
@@ -436,13 +434,11 @@
     out_ref[...] = packed + jnp.where(line == 12 + subtree, length_row, 0.0)
 
 
-def last_kernel(total_sites, parts_ref, exch_ref, omega_ref, length_ref, log_ref):
+def last_kernel(total_sites, count, *refs):
     members = lax.axis_size("branch")
     subtree = lax.axis_index("branch")
-    devices = parts_ref.shape[0]
-    total = parts_ref[0]
-    for device in range(1, devices):
-        total = total + parts_ref[device]
+    exch_ref, omega_ref, length_ref, log_ref = refs[count:]
+    total = tree_sum([ref[...] for ref in refs[:count]])
     masks, picks = neighbours()
     table = jnp.zeros((64, 128), F32)
     for at_position, pick in zip(masks, picks):
@@ -454,6 +450,30 @@
     lengths = jnp.sum(jnp.where(line == 12 + subtree, total, 0.0), axis=0, keepdims=True)
     length_ref[...] = lengths[:, 0:EDGES]
     log_ref[...] = moved[0:1, CLASSES : CLASSES + 1] / total_sites / (LEAF_DEV * members)
+
+
+def partners(x, axis, start, radix):
+    size = lax.axis_size(axis)
+    others = [
+        lax.ppermute(x, axis, [(i, i ^ (step * start)) for i in range(size)])
+        for step in range(1, radix)
+    ]
+    return [x] + others
+
+
+def tree_sum(parts):
+    while len(parts) > 1:
+        parts = [parts[i] + parts[i + 1] for i in range(0, len(parts), 2)]
+    return parts[0]
+
+
+def axis_steps(axis):
+    size, start, steps = lax.axis_size(axis), 1, []
+    while start < size:
+        radix = min(8, size // start)
+        steps.append((axis, start, radix))
+        start *= radix
+    return steps
 
 
 def body(
@@ -495,11 +515,11 @@
         sense2, single2, nonsyn2,
     )
     kept = [pltpu.with_memory_space_constraint(x, pltpu.VMEM) for x in kept]
-    tops = lax.all_gather(top, "branch", axis=0, tiled=True)
+    tops = partners(top, "branch", 1, members)
     part = pl.pallas_call(
-        functools.partial(down_kernel, total_sites),
+        functools.partial(down_kernel, total_sites, members),
         out_shape=shape((16, 128), F32),
-        in_specs=[vmem] * 13 + [smem] * 3 + [vmem] * 3,
+        in_specs=[vmem] * (12 + members) + [smem] * 3 + [vmem] * 3,
         out_specs=vmem,
         scratch_shapes=[
             pltpu.VMEM((32, 128, sites), BF),
@@ -511,18 +531,21 @@
         compiler_params=pltpu.CompilerParams(vmem_limit_bytes=28 * 2**20),
         name="down",
     )(
-        tops, *kept, weights.reshape(1, sites), exchanges, freq, omega_ratio, lengths, classes,
+        *tops, *kept, weights.reshape(1, sites), exchanges, freq, omega_ratio, lengths, classes,
         sense2, single2, nonsyn2,
     )
-    parts = lax.all_gather(part, ("site", "branch"), axis=0)
+    steps = axis_steps("branch") + axis_steps("site")
+    for step in steps[:-1]:
+        part = tree_sum(partners(part, *step))
+    parts = partners(part, *steps[-1])
     exch, omega, length, loglik = pl.pallas_call(
-        functools.partial(last_kernel, total_sites),
+        functools.partial(last_kernel, total_sites, len(parts)),
         out_shape=[shape((64, 64), F32), shape((1, CLASSES), F32), shape((1, EDGES), F32), shape((1, 1), F32)],
-        in_specs=[vmem],
+        in_specs=[vmem] * len(parts),
         out_specs=[vmem] * 4,
         compiler_params=pltpu.CompilerParams(vmem_limit_bytes=24 * 2**20),
         name="last",
-    )(parts)
+    )(*parts)
     return (exch, omega.reshape(CLASSES), length.reshape(EDGES), loglik.reshape(()))
 
 

time: 96.6 us -> 74.2 us (0.77)
  blocking collectives: 50.6 us -> 0 us
  starting transfers between devices: 0 us -> 16.1 us
  waiting for transfers between devices: 0 us -> 10.8 us
    all_gather x2 -> x0, blocking collectives: 50.6 us -> none  [the longest x1 41.8 us: body(): parts = lax.all_gather(part, ('site', 'branch'), axis=0)]
    ppermute x0 -> x13, starting transfers between devices: none -> 16.1 us  [partners(): lax.ppermute(x, axis, [(i, i ^ step * start) for i in range(size)])]
    ppermute x0 -> x13, waiting for transfers between devices: none -> 10.8 us  [partners(): lax.ppermute(x, axis, [(i, i ^ step * start) for i in range(size)])]
  transfers between devices with their start and end apart: 0 -> 13, of which waited for: 0 -> 7; matrix products, arithmetic and copies ran while one was open for 0% -> 0% of each run, Pallas kernels for 0% -> 0%
where the time goes in v1:
time: 74.2 us; the launch traced here: 73.9 us
  Pallas kernels  45.1 us (61%)
  starting transfers between devices  16.1 us (22%)
  waiting for transfers between devices  10.8 us (15%)
    pallas_call x1, Pallas kernels, body(): pl.pallas_call(functools.partial(down_kernel, total_sites, members), out_...  24.8 us
    pallas_call x1, Pallas kernels, body(): pl.pallas_call(up_kernel, out_shape=[shape((64, sites), F32), held((5, PA...  19.5 us
    ppermute x13, starting transfers between devices, partners(): lax.ppermute(x, axis, [(i, i ^ step * start) for i in range(size)])  16.1 us
    ppermute x13, waiting for transfers between devices, partners(): lax.ppermute(x, axis, [(i, i ^ step * start) for i in range(size)])  10.8 us
  transfers between devices with their start and end apart: 13, of which 7 were waited for; matrix products, arithmetic and copies ran while one was open for 0% of the time, Pallas kernels for 0%

profile of v1, /device:TPU:0, one launch (start us, length us, event | category | flops | bytes accessed | tf_op | source)
XLA Modules:
  0.0 73.9 jit_solution(12994626514220368396)
XLA Ops:
  0.6 19.5 %up.1 = (f32[64,256]{1,0:T(8,128)}, f32[5,64,64,128]{3,2,1,0:T(8,128)S(1)}, f32[64,64,128]{2,1,0:T(8,128)S(1)}, f32[4,4,64,128]{3,2,1,0:T(8,128)S(1)}, f32[64,12...) custom-call(s32[256,256]{1,0:T(8,128)} %states_ref.1, ...), custom_call_target="tpu_custom_call" | custom-call | tf_op jit(solution)/shard_map/up/pallas_call | solution.py:494
  20.1 2.4 %collective-permute-start.2 = (f32[64,256]{1,0:T(8,128)}, f32[64,256]{1,0:T(8,128)S(1)}, u32[]{:S(2)}, u32[]{:S(2)}) collective-permute-start(f32[64,256]{1,0:T(8,128)} %get-tuple-element.18.refs_0_), channel_id=1, source_target_pairs={{0,3},{1,2},{2,1},{3,0},{4,7},{5,6},{6,5},{7,4},{8,11},{9,10},{10,... | collective-permute-start | bytes 196616 | tf_op jit(solution)/shard_map/ppermute | solution.py:458
  22.5 0.6 collective-permute-start.1
  23.1 0.1 collective-permute-start
  23.2 2.1 %collective-permute-done.2.refs_3_ = f32[64,256]{1,0:T(8,128)S(1)} collective-permute-done((f32[64,256]{1,0:T(8,128)}, f32[64,256]{1,0:T(8,128)S(1)}, u32[]{:S(2)}, u32[]{:S(2)}) %collective-permute-start.2) | collective-permute-done | bytes 65568 | tf_op jit(solution)/shard_map/ppermute | solution.py:458
  25.3 0.0 copy-start
  25.3 2.1 %collective-permute-done.1.refs_2_ = f32[64,256]{1,0:T(8,128)S(1)} collective-permute-done((f32[64,256]{1,0:T(8,128)}, f32[64,256]{1,0:T(8,128)S(1)}, u32[]{:S(2)}, u32[]{:S(2)}) %collective-permute-start.1) | collective-permute-done | bytes 65568 | tf_op jit(solution)/shard_map/ppermute | solution.py:458
  27.4 0.0 copy-start.1
  27.4 0.0 collective-permute-done.refs_1_
  27.4 0.0 copy-start.2
  27.4 0.0 copy-done
  27.4 0.6 copy-done.1
  28.0 0.0 copy-done.2
  28.0 24.8 %down.1 = f32[16,128]{1,0:T(8,128)} custom-call(f32[64,256]{1,0:T(8,128)} %get-tuple-element.18.refs_0_, f32[64,256]{1,0:T(8,128)} %copy-done.2, f32[64,256]{1,0:T(8,128)} %copy-done.1, f32[64,256]{1,0:T(8,128)} %copy-done, f32[5,64,64,128]{3,2,1,0:T(8,128)S(1)} %get-tuple-element.19.refs_4_, f32[64,64,128]{2,1,0:T(8,128)S(1)} %get-tuple-element.20.refs_5_, ...), custom_call_target="tpu_custom_call" | custom-call | tf_op jit(solution)/shard_map/down/pallas_call | solution.py:519
  52.8 1.4 %collective-permute-start.5 = (f32[16,128]{1,0:T(8,128)}, f32[16,128]{1,0:T(8,128)S(1)}, u32[]{:S(2)}, u32[]{:S(2)}) collective-permute-start(f32[16,128]{1,0:T(8,128)} %down.1), channel_id=1, source_target_pairs={{0,3},{1,2},{2,1},{3,0},{4,7},{5,6},{6,5},{7,4},{8,11},{9,10},{10,... | collective-permute-start | bytes 24584 | tf_op jit(solution)/shard_map/ppermute | solution.py:458
  54.2 0.3 collective-permute-start.4
  54.5 0.2 collective-permute-start.3
  54.7 1.4 %collective-permute-done.5 = f32[16,128]{1,0:T(8,128)S(1)} collective-permute-done((f32[16,128]{1,0:T(8,128)}, f32[16,128]{1,0:T(8,128)S(1)}, u32[]{:S(2)}, u32[]{:S(2)}) %collective-permute-start.5) | collective-permute-done | bytes 8224 | tf_op jit(solution)/shard_map/ppermute | solution.py:458
  56.1 2.0 %collective-permute-done.4 = f32[16,128]{1,0:T(8,128)S(1)} collective-permute-done((f32[16,128]{1,0:T(8,128)}, f32[16,128]{1,0:T(8,128)S(1)}, u32[]{:S(2)}, u32[]{:S(2)}) %collective-permute-start.4) | collective-permute-done | bytes 8224 | tf_op jit(solution)/shard_map/ppermute | solution.py:458
  58.1 0.0 collective-permute-done.3
  58.1 0.7 add_add_fusion.refs_0_
  58.8 4.6 %collective-permute-start.12 = (f32[16,128]{1,0:T(8,128)S(1)}, f32[16,128]{1,0:T(8,128)S(1)}, u32[]{:S(2)}, u32[]{:S(2)}) collective-permute-start(f32[16,128]{1,0:T(8,128)S(1)} %add_add_fusion.refs_0_), channel_id=1, source_target_pairs={{0,28},{4,24},{8,20},{12,16},{16,12},{20,8},{24,4},{28,0},{1,29},{... | collective-permute-start | bytes 24584 | tf_op jit(solution)/shard_map/ppermute | solution.py:458
  63.4 0.2 collective-permute-start.11
  63.6 0.7 collective-permute-start.10
  64.3 2.1 %collective-permute-start.9 = (f32[16,128]{1,0:T(8,128)S(1)}, f32[16,128]{1,0:T(8,128)S(1)}, u32[]{:S(2)}, u32[]{:S(2)}) collective-permute-start(f32[16,128]{1,0:T(8,128)S(1)} %add_add_fusion.refs_0_), channel_id=1, source_target_pairs={{0,16},{4,20},{8,24},{12,28},{16,0},{20,4},{24,8},{28,12},{1,17},{... | collective-permute-start | bytes 24584 | tf_op jit(solution)/shard_map/ppermute | solution.py:458
  66.5 2.2 %collective-permute-start.8 = (f32[16,128]{1,0:T(8,128)S(1)}, f32[16,128]{1,0:T(8,128)S(1)}, u32[]{:S(2)}, u32[]{:S(2)}) collective-permute-start(f32[16,128]{1,0:T(8,128)S(1)} %add_add_fusion.refs_0_), channel_id=1, source_target_pairs={{0,12},{4,8},{8,4},{12,0},{16,28},{20,24},{24,20},{28,16},{1,13},{... | collective-permute-start | bytes 24584 | tf_op jit(solution)/shard_map/ppermute | solution.py:458
  68.7 0.0 collective-permute-done.12.refs_7_
  68.7 0.8 %collective-permute-start.7 = (f32[16,128]{1,0:T(8,128)S(1)}, f32[16,128]{1,0:T(8,128)S(1)}, u32[]{:S(2)}, u32[]{:S(2)}) collective-permute-start(f32[16,128]{1,0:T(8,128)S(1)} %add_add_fusion.refs_0_), channel_id=1, source_target_pairs={{0,8},{4,12},{8,0},{12,4},{16,24},{20,28},{24,16},{28,20},{1,9},{5... | collective-permute-start | bytes 24584 | tf_op jit(solution)/shard_map/ppermute | solution.py:458
  69.5 0.0 collective-permute-done.11.refs_6_
  69.5 0.5 collective-permute-start.6
  70.0 0.0 collective-permute-done.10.refs_5_
  70.0 0.0 collective-permute-done.9.refs_4_
  70.0 1.0 %collective-permute-done.8.refs_3_ = f32[16,128]{1,0:T(8,128)S(1)} collective-permute-done((f32[16,128]{1,0:T(8,128)S(1)}, f32[16,128]{1,0:T(8,128)S(1)}, u32[]{:S(2)}, u32[]{:S(2)}) %collective-permute-start.8) | collective-permute-done | bytes 8224 | tf_op jit(solution)/shard_map/ppermute | solution.py:458
  71.0 1.3 %collective-permute-done.7.refs_2_ = f32[16,128]{1,0:T(8,128)S(1)} collective-permute-done((f32[16,128]{1,0:T(8,128)S(1)}, f32[16,128]{1,0:T(8,128)S(1)}, u32[]{:S(2)}, u32[]{:S(2)}) %collective-permute-start.7) | collective-permute-done | bytes 8224 | tf_op jit(solution)/shard_map/ppermute | solution.py:458
  72.3 0.8 %collective-permute-done.6.refs_1_ = f32[16,128]{1,0:T(8,128)S(1)} collective-permute-done((f32[16,128]{1,0:T(8,128)S(1)}, f32[16,128]{1,0:T(8,128)S(1)}, u32[]{:S(2)}, u32[]{:S(2)}) %collective-permute-start.6) | collective-permute-done | bytes 8224 | tf_op jit(solution)/shard_map/ppermute | solution.py:458
  73.1 0.8 %last.1 = (f32[64,64]{1,0:T(8,128)}, f32[1,8]{1,0:T(1,128)}, f32[1,127]{1,0:T(1,128)}, f32[1,1]{1,0:T(1,128)}) custom-call(f32[16,128]{1,0:T(8,128)S(1)} %add_add_fusion.refs_0_, f32[16,128]{1,0:T(8,128)S(1)} %collective-permute-done.6.refs_1_, f32[16,128]{1,0:T(8,128)S(1)} %collective-permute-done.7.refs_2_, f32[16,128]{1,0:T(8,128)S(1)} %collective-permute-done.8.refs_3_, ...), custom_call_target="tpu_custom_call" | custom-call | tf_op jit(solution)/shard_map/last/pallas_call | solution.py:541
Async XLA Ops:
  20.1 5.2 %collective-permute-start.2 = (f32[64,256]{1,0:T(8,128)}, f32[64,256]{1,0:T(8,128)S(1)}, u32[]{:S(2)}, u32[]{:S(2)}) collective-permute-start(f32[64,256]{1,0:T(8,128)} %get-tuple-element.18.refs_0_), channel_id=1, source_target_pairs={{0,3},{1,2},{2,1},{3,0},{4,7},{5,6},{6,5},{7,4},{8,11},{9,10},{10,... | collective-permute-start | bytes 196616 | tf_op jit(solution)/shard_map/ppermute | solution.py:458
  22.5 4.9 %collective-permute-start.1 = (f32[64,256]{1,0:T(8,128)}, f32[64,256]{1,0:T(8,128)S(1)}, u32[]{:S(2)}, u32[]{:S(2)}) collective-permute-start(f32[64,256]{1,0:T(8,128)} %get-tuple-element.18.refs_0_), channel_id=1, source_target_pairs={{0,2},{1,3},{2,0},{3,1},{4,6},{5,7},{6,4},{7,5},{8,10},{9,11},{10,... | collective-permute-start | bytes 196616 | tf_op jit(solution)/shard_map/ppermute | solution.py:458
  23.1 4.3 %collective-permute-start = (f32[64,256]{1,0:T(8,128)}, f32[64,256]{1,0:T(8,128)S(1)}, u32[]{:S(2)}, u32[]{:S(2)}) collective-permute-start(f32[64,256]{1,0:T(8,128)} %get-tuple-element.18.refs_0_), channel_id=1, source_target_pairs={{0,1},{1,0},{2,3},{3,2},{4,5},{5,4},{6,7},{7,6},{8,9},{9,8},{10,11... | collective-permute-start | bytes 196616 | tf_op jit(solution)/shard_map/ppermute | solution.py:458
  25.3 2.1 %copy-start = (f32[64,256]{1,0:T(8,128)}, f32[64,256]{1,0:T(8,128)S(1)}, u32[]{:S(2)}) copy-start(f32[64,256]{1,0:T(8,128)S(1)} %collective-permute-done.2.refs_3_) | copy-start | bytes 196612
  27.4 0.6 copy-start.1
  27.4 0.6 copy-start.2
  52.8 3.3 %collective-permute-start.5 = (f32[16,128]{1,0:T(8,128)}, f32[16,128]{1,0:T(8,128)S(1)}, u32[]{:S(2)}, u32[]{:S(2)}) collective-permute-start(f32[16,128]{1,0:T(8,128)} %down.1), channel_id=1, source_target_pairs={{0,3},{1,2},{2,1},{3,0},{4,7},{5,6},{6,5},{7,4},{8,11},{9,10},{10,... | collective-permute-start | bytes 24584 | tf_op jit(solution)/shard_map/ppermute | solution.py:458
  54.2 3.9 %collective-permute-start.4 = (f32[16,128]{1,0:T(8,128)}, f32[16,128]{1,0:T(8,128)S(1)}, u32[]{:S(2)}, u32[]{:S(2)}) collective-permute-start(f32[16,128]{1,0:T(8,128)} %down.1), channel_id=1, source_target_pairs={{0,2},{1,3},{2,0},{3,1},{4,6},{5,7},{6,4},{7,5},{8,10},{9,11},{10,... | collective-permute-start | bytes 24584 | tf_op jit(solution)/shard_map/ppermute | solution.py:458
  54.5 3.6 %collective-permute-start.3 = (f32[16,128]{1,0:T(8,128)}, f32[16,128]{1,0:T(8,128)S(1)}, u32[]{:S(2)}, u32[]{:S(2)}) collective-permute-start(f32[16,128]{1,0:T(8,128)} %down.1), channel_id=1, source_target_pairs={{0,1},{1,0},{2,3},{3,2},{4,5},{5,4},{6,7},{7,6},{8,9},{9,8},{10,11... | collective-permute-start | bytes 24584 | tf_op jit(solution)/shard_map/ppermute | solution.py:458
  58.8 9.9 %collective-permute-start.12 = (f32[16,128]{1,0:T(8,128)S(1)}, f32[16,128]{1,0:T(8,128)S(1)}, u32[]{:S(2)}, u32[]{:S(2)}) collective-permute-start(f32[16,128]{1,0:T(8,128)S(1)} %add_add_fusion.refs_0_), channel_id=1, source_target_pairs={{0,28},{4,24},{8,20},{12,16},{16,12},{20,8},{24,4},{28,0},{1,29},{... | collective-permute-start | bytes 24584 | tf_op jit(solution)/shard_map/ppermute | solution.py:458
  63.4 6.1 %collective-permute-start.11 = (f32[16,128]{1,0:T(8,128)S(1)}, f32[16,128]{1,0:T(8,128)S(1)}, u32[]{:S(2)}, u32[]{:S(2)}) collective-permute-start(f32[16,128]{1,0:T(8,128)S(1)} %add_add_fusion.refs_0_), channel_id=1, source_target_pairs={{0,24},{4,28},{8,16},{12,20},{16,8},{20,12},{24,0},{28,4},{1,25},{... | collective-permute-start | bytes 24584 | tf_op jit(solution)/shard_map/ppermute | solution.py:458
  63.6 6.4 %collective-permute-start.10 = (f32[16,128]{1,0:T(8,128)S(1)}, f32[16,128]{1,0:T(8,128)S(1)}, u32[]{:S(2)}, u32[]{:S(2)}) collective-permute-start(f32[16,128]{1,0:T(8,128)S(1)} %add_add_fusion.refs_0_), channel_id=1, source_target_pairs={{0,20},{4,16},{8,28},{12,24},{16,4},{20,0},{24,12},{28,8},{1,21},{... | collective-permute-start | bytes 24584 | tf_op jit(solution)/shard_map/ppermute | solution.py:458
  64.3 5.6 %collective-permute-start.9 = (f32[16,128]{1,0:T(8,128)S(1)}, f32[16,128]{1,0:T(8,128)S(1)}, u32[]{:S(2)}, u32[]{:S(2)}) collective-permute-start(f32[16,128]{1,0:T(8,128)S(1)} %add_add_fusion.refs_0_), channel_id=1, source_target_pairs={{0,16},{4,20},{8,24},{12,28},{16,0},{20,4},{24,8},{28,12},{1,17},{... | collective-permute-start | bytes 24584 | tf_op jit(solution)/shard_map/ppermute | solution.py:458
  66.5 4.5 %collective-permute-start.8 = (f32[16,128]{1,0:T(8,128)S(1)}, f32[16,128]{1,0:T(8,128)S(1)}, u32[]{:S(2)}, u32[]{:S(2)}) collective-permute-start(f32[16,128]{1,0:T(8,128)S(1)} %add_add_fusion.refs_0_), channel_id=1, source_target_pairs={{0,12},{4,8},{8,4},{12,0},{16,28},{20,24},{24,20},{28,16},{1,13},{... | collective-permute-start | bytes 24584 | tf_op jit(solution)/shard_map/ppermute | solution.py:458
  68.7 3.7 %collective-permute-start.7 = (f32[16,128]{1,0:T(8,128)S(1)}, f32[16,128]{1,0:T(8,128)S(1)}, u32[]{:S(2)}, u32[]{:S(2)}) collective-permute-start(f32[16,128]{1,0:T(8,128)S(1)} %add_add_fusion.refs_0_), channel_id=1, source_target_pairs={{0,8},{4,12},{8,0},{12,4},{16,24},{20,28},{24,16},{28,20},{1,9},{5... | collective-permute-start | bytes 24584 | tf_op jit(solution)/shard_map/ppermute | solution.py:458
  69.5 3.7 %collective-permute-start.6 = (f32[16,128]{1,0:T(8,128)S(1)}, f32[16,128]{1,0:T(8,128)S(1)}, u32[]{:S(2)}, u32[]{:S(2)}) collective-permute-start(f32[16,128]{1,0:T(8,128)S(1)} %add_add_fusion.refs_0_), channel_id=1, source_target_pairs={{0,4},{4,0},{8,12},{12,8},{16,20},{20,16},{24,28},{28,24},{1,5},{5... | collective-permute-start | bytes 24584 | tf_op jit(solution)/shard_map/ppermute | solution.py:458

commit v2 on v0

--- a/solution.py
+++ b/solution.py
@@ -255,7 +255,8 @@
     inverse_ref[63:64, :] = jnp.ones((1, sites), F32)
     top = inner(63)
     message_ref[63] = top
-    top_ref[...] = top[0:64]
+    for member in range(top_ref.shape[0]):
+        top_ref[member] = top[0:64]
 
 
 def down_kernel(
@@ -267,7 +268,6 @@
     a_high_ref, a_low_ref, count_ref, bins_ref, dot_ref,
 ):
     subtree = lax.axis_index("branch")
-    members = lax.axis_size("branch")
     mask = low_half()
     twice, pi_row, pi_col, root_row, root_col = frequencies(freq_ref, sense_ref)
     inverse_root_row, inverse_root_col = 1.0 / root_row, 1.0 / root_col
@@ -276,8 +276,8 @@
 
     above = jnp.broadcast_to(pi_col, (64, sites))
     own = jnp.zeros((64, sites), F32)
-    for member in range(members):
-        message = tops_ref[member * 64 : member * 64 + 64, :]
+    for member in range(tops_ref.shape[0]):
+        message = tops_ref[member]
         above = jnp.where(subtree == member, above, above * message)
         own = jnp.where(subtree == member, message, own)
     likelihood = jnp.sum(above * own, axis=0, keepdims=True)
@@ -429,20 +429,19 @@
     other = jnp.sum(jnp.where(mask, 0.0, slopes), axis=1, keepdims=True)
     placed = jnp.where(lane == 2 * row, even, 0.0) + jnp.where(lane == 2 * row + 1, other, 0.0)
     length_row = jnp.sum(placed, axis=0, keepdims=True)
-    line = lax.broadcasted_iota(jnp.int32, out_ref.shape, 0)
+    line = lax.broadcasted_iota(jnp.int32, packed.shape, 0)
     omega_row = jnp.where(lane_row == CLASSES, log_part, omega_row)
     omega_row = pltpu.roll(jnp.broadcast_to(omega_row, (8, 128)), 64, 1)[0:1]
     packed = packed + jnp.where(line == 0, omega_row, 0.0)
-    out_ref[...] = packed + jnp.where(line == 12 + subtree, length_row, 0.0)
+    packed = packed + jnp.where(line == 12 + subtree, length_row, 0.0)
+    for device in range(out_ref.shape[0]):
+        out_ref[device] = packed
 
 
 def last_kernel(total_sites, parts_ref, exch_ref, omega_ref, length_ref, log_ref):
     members = lax.axis_size("branch")
     subtree = lax.axis_index("branch")
-    devices = parts_ref.shape[0]
-    total = parts_ref[0]
-    for device in range(1, devices):
-        total = total + parts_ref[device]
+    total = tree_sum([parts_ref[device] for device in range(parts_ref.shape[0])])
     masks, picks = neighbours()
     table = jnp.zeros((64, 128), F32)
     for at_position, pick in zip(masks, picks):
@@ -456,12 +455,19 @@
     log_ref[...] = moved[0:1, CLASSES : CLASSES + 1] / total_sites / (LEAF_DEV * members)
 
 
+def tree_sum(parts):
+    while len(parts) > 1:
+        parts = [parts[i] + parts[i + 1] for i in range(0, len(parts), 2)]
+    return parts[0]
+
+
 def body(
     total_sites, states, gap_mask, weights, leaf_order, exchanges, codon_freq, omega_ratio,
     lengths, classes,
 ):
     sites = states.shape[1]
     members = lax.axis_size("branch")
+    devices = members * lax.axis_size("site")
     sense, single, nonsyn = codon_tables()
     sense2 = jnp.asarray(np.tile(sense[None, :], (1, 2)))
     single2 = jnp.asarray(np.tile(single, (1, 2)))
@@ -474,7 +480,7 @@
     top, *kept = pl.pallas_call(
         up_kernel,
         out_shape=[
-            shape((64, sites), F32),
+            shape((members, 64, sites), F32),
             held((5, PAIRS, 64, 128), F32),
             held((PAIRS, 64, 128), F32),
             held((CLASSES // 2, 4, 64, 128), F32),
@@ -495,10 +501,10 @@
         sense2, single2, nonsyn2,
     )
     kept = [pltpu.with_memory_space_constraint(x, pltpu.VMEM) for x in kept]
-    tops = lax.all_gather(top, "branch", axis=0, tiled=True)
+    tops = lax.all_to_all(top, "branch", 0, 0, tiled=True)
     part = pl.pallas_call(
         functools.partial(down_kernel, total_sites),
-        out_shape=shape((16, 128), F32),
+        out_shape=shape((devices, 16, 128), F32),
         in_specs=[vmem] * 13 + [smem] * 3 + [vmem] * 3,
         out_specs=vmem,
         scratch_shapes=[
@@ -514,7 +520,7 @@
         tops, *kept, weights.reshape(1, sites), exchanges, freq, omega_ratio, lengths, classes,
         sense2, single2, nonsyn2,
     )
-    parts = lax.all_gather(part, ("site", "branch"), axis=0)
+    parts = lax.all_to_all(part, ("site", "branch"), 0, 0, tiled=True)
     exch, omega, length, loglik = pl.pallas_call(
         functools.partial(last_kernel, total_sites),
         out_shape=[shape((64, 64), F32), shape((1, CLASSES), F32), shape((1, EDGES), F32), shape((1, 1), F32)],

time: 96.6 us -> 73.5 us (0.76)
  blocking collectives: 50.6 us -> 27.1 us
    all_gather x2 -> x0, blocking collectives: 50.6 us -> none  [the longest x1 41.8 us: body(): parts = lax.all_gather(part, ('site', 'branch'), axis=0)]
    all_to_all x0 -> x2, blocking collectives: none -> 27.1 us  [the longest x1 16.4 us: body(): parts = lax.all_to_all(part, ('site', 'branch'), 0, 0, tiled=True)]
where the time goes in v2:
time: 73.5 us; the launch traced here: 73.2 us
  Pallas kernels  45.4 us (62%)
  blocking collectives  27.1 us (37%)
    pallas_call x1, Pallas kernels, body(): pl.pallas_call(functools.partial(down_kernel, total_sites), out_shape=sha...  25 us
    pallas_call x1, Pallas kernels, body(): pl.pallas_call(up_kernel, out_shape=[shape((members, 64, sites), F32), he...  19.6 us
    all_to_all x1, blocking collectives, body(): parts = lax.all_to_all(part, ('site', 'branch'), 0, 0, tiled=True)  16.4 us
    all_to_all x1, blocking collectives, body(): tops = lax.all_to_all(top, 'branch', 0, 0, tiled=True)  10.8 us

profile of v2, /device:TPU:0, one launch (start us, length us, event | category | flops | bytes accessed | tf_op | source)
XLA Modules:
  0.0 73.2 jit_solution(5220479862393093438)
XLA Ops:
  0.6 19.6 %up.1 = (f32[4,64,256]{2,1,0:T(8,128)}, f32[5,64,64,128]{3,2,1,0:T(8,128)S(1)}, f32[64,64,128]{2,1,0:T(8,128)S(1)}, f32[4,4,64,128]{3,2,1,0:T(8,128)S(1)}, f32[6...) custom-call(s32[256,256]{1,0:T(8,128)} %states_ref.1, ...), custom_call_target="tpu_custom_call" | custom-call | tf_op jit(solution)/shard_map/up/pallas_call | solution.py:480
  20.2 10.8 %all_to_all.10.tops_ref = f32[4,64,256]{2,1,0:T(8,128)} all-to-all(f32[4,64,256]{2,1,0:T(8,128)} %get-tuple-element.18), channel_id=1, replica_groups=mesh['site'=8,'branch'=4] {'branch'}, dimensions={0} | all-to-all | bytes 524288 | tf_op jit(solution)/shard_map/all_to_all | solution.py:504
  31.0 25.0 %down.1 = f32[32,16,128]{2,1,0:T(8,128)} custom-call(f32[4,64,256]{2,1,0:T(8,128)} %all_to_all.10.tops_ref, f32[5,64,64,128]{3,2,1,0:T(8,128)S(1)} %get-tuple-element.19.chain_ref, f32[64,64,128]{2,1,0:T(8,128)S(1)} %get-tuple-element.20.slope_ref, f32[4,4,64,128]{3,2,1,0:T(8,128)S(1)} %get-tuple-element.21.power_ref, ...), custom_call_target="tpu_custom_call" | custom-call | tf_op jit(solution)/shard_map/down/pallas_call | solution.py:505
  56.0 16.4 %all_to_all.11.parts_ref = f32[32,16,128]{2,1,0:T(8,128)S(1)} all-to-all(f32[32,16,128]{2,1,0:T(8,128)} %down.1), channel_id=1, replica_groups=mesh['site'=8,'branch'=4] {'site','branch'}, dimensions={0} | all-to-all | bytes 524288 | tf_op jit(solution)/shard_map/all_to_all | solution.py:523
  72.3 0.9 %last.1 = (f32[64,64]{1,0:T(8,128)}, f32[1,8]{1,0:T(1,128)}, f32[1,127]{1,0:T(1,128)}, f32[1,1]{1,0:T(1,128)}) custom-call(f32[32,16,128]{2,1,0:T(8,128)S(1)} %all_to_all.11.parts_ref), custom_call_target="tpu_custom_call" | custom-call | tf_op jit(solution)/shard_map/last/pallas_call | solution.py:524
